TPU v7x, 512 devices: a whole 4x4x16 slice. The times are simulated.
512 devices in a mesh: blk: 256 (over y, x_lo, z, core), rep: 2 (over x_hi).
Axes of the slice: x: 4 (x_hi: 2, x_lo: 2; x = x_hi * 2 + x_lo), y: 4, z: 16, core: 2. Of those that a mesh axis runs over, the one named last changes fastest.
Arguments:
- images: bfloat16 [2, 98304, 1024], P('rep', 'blk'), may hold values from -27 to 27
- texts: bfloat16 [2, 98304, 1024], P('rep', 'blk'), may hold values from -27 to 27
- log_scale: float32 [], replicated, may hold values from -2.6 to -2
Outputs:
- grad_image: bfloat16 [2, 98304, 1024], P('rep', 'blk')
- grad_text: bfloat16 [2, 98304, 1024], P('rep', 'blk')
- loss: float32 [], replicated
- grad_scale: float32 [], replicated
All inputs are finite; a program needn't handle non-finite values.
Results may differ from a plain program's by a relative error of at most 0.0041.
Values may be sent and summed in bfloat16 or wider, within the bound.
A program may use at most 64 MiB of HBM per device.

v0:
```python
import jax
import jax.numpy as jnp
from jax import lax
from jax.sharding import PartitionSpec as P

HOPS = 4


def shifted(array, axis, by):
    peers = lax.axis_size(axis)
    return lax.ppermute(array, axis, [(i, (i + by) % peers) for i in range(peers)])


def pair_scores(scale, left_rows, right_rows):
    return scale * lax.dot_general(
        left_rows, right_rows, (((1,), (1,)), ((), ())), preferred_element_type=jnp.float32
    )


def body(images, texts, log_scale):
    image_rows = images[0]
    own_text = texts[0]
    scale = jnp.exp(log_scale)
    row_count = image_rows.shape[0]
    identity = jnp.eye(row_count, dtype=jnp.float32)
    image_acc = jnp.zeros(image_rows.shape, jnp.float32)
    text_acc = jnp.zeros(image_rows.shape, jnp.float32)
    scale_sum = jnp.zeros((), jnp.float32)
    first_tile = pair_scores(scale, image_rows, own_text)
    diagonal = jnp.diagonal(first_tile)
    row_lse = jax.nn.logsumexp(first_tile, axis=1)
    column_lse = jax.nn.logsumexp(first_tile, axis=0)
    current = own_text
    for offset in range(1, HOPS + 1):
        current = shifted(current, "blk", 1)
        column_lse = shifted(column_lse, "blk", 1)
        logits = pair_scores(scale, image_rows, current)
        row_lse = jnp.logaddexp(row_lse, jax.nn.logsumexp(logits, axis=1))
        column_lse = jnp.logaddexp(column_lse, jax.nn.logsumexp(logits, axis=0))
    for section in range(HOPS + 1):
        offset = HOPS - section
        block = current
        logits = pair_scores(scale, image_rows, block)
        weights = 0.5 * (jnp.exp(logits - row_lse[:, None]) + jnp.exp(logits - column_lse[None, :]))
        if offset == 0:
            weights = weights - identity
        rounded = weights.astype(jnp.bfloat16)
        image_acc = image_acc + jnp.dot(rounded, block, preferred_element_type=jnp.float32)
        text_acc = text_acc + lax.dot_general(
            rounded, image_rows, (((0,), (0,)), ((), ())), preferred_element_type=jnp.float32
        )
        scale_sum = scale_sum + jnp.sum(weights * logits)
        if section < HOPS:
            text_acc, column_lse = shifted((text_acc, column_lse), "blk", -1)
            current = shifted(current, "blk", -1)
    loss_part = jnp.sum(row_lse - diagonal) + jnp.sum(column_lse - diagonal)
    loss_total, scale_total = lax.psum((loss_part, scale_sum), ("blk", "rep"))
    count = lax.axis_size("blk") * lax.axis_size("rep") * row_count
    grad_img = (scale * image_acc).astype(jnp.bfloat16)[None]
    grad_txt = (scale * text_acc).astype(jnp.bfloat16)[None]
    return (grad_img, grad_txt, 0.5 * loss_total / count, scale_total / count)


def solution(mesh):
    placed = (P("rep", "blk", None), P("rep", "blk", None), P())
    return jax.shard_map(
        body,
        mesh=mesh,
        in_specs=placed,
        out_specs=(P("rep", "blk", None), P("rep", "blk", None), P(), P()),
        check_vma=False,
    )
```

profile of v0, /device:TPU:1, one launch (start us, length us, event | category | flops | bytes accessed | tf_op | source)
XLA Modules:
  0.0 361.3 jit_solution(5315833872368255656)
XLA Ops:
  0.6 0.0 copy-start
  0.6 5.1 %collective-permute-start = (bf16[384,1024]{1,0:T(8,128)(2,1)}, bf16[384,1024]{1,0:T(8,128)(2,1)S(1)}, u32[]{:S(2)}, u32[]{:S(2)}) collective-permute-start(bf16[384,1024]{1,0:T(8,128)(2,1)} %bitcast.69), channel_id=1, source_target_pairs={{0,2},{2,4},{4,6},{6,8},{8,10},{10,12},{12,14},{14,16},{16,18},{18... | collective-permute-start | bytes 2359304 | tf_op jit(solution)/shard_map/ppermute | solution.py:11
  6.4 1.8 fusion.55
  8.2 0.3 exponential_reduce_fusion.9
  8.5 1.9 collective-permute-start.4
  10.5 4.5 %collective-permute-done = bf16[384,1024]{1,0:T(8,128)(2,1)S(1)} collective-permute-done((bf16[384,1024]{1,0:T(8,128)(2,1)}, bf16[384,1024]{1,0:T(8,128)(2,1)S(1)}, u32[]{:S(2)}, u32[]{:S(2)}) %collective-permute-start) | collective-permute-done | bytes 786464 | tf_op jit(solution)/shard_map/ppermute | solution.py:11
  14.9 4.3 %collective-permute-start.1 = (bf16[384,1024]{1,0:T(8,128)(2,1)S(1)}, bf16[384,1024]{1,0:T(8,128)(2,1)S(1)}, u32[]{:S(2)}, u32[]{:S(2)}) collective-permute-start(bf16[384,1024]{1,0:T(8,128)(2,1)S(1)} %collective-permute-done), channel_id=1, source_target_pairs={{0,2},{2,4},{4,6},{6,8},{8,10},{10,12},{12,14},{14,16},{16,18},{18... | collective-permute-start | bytes 2359304 | tf_op jit(solution)/shard_map/ppermute | solution.py:11
  19.2 0.7 fusion.54
  19.9 0.3 exponential_reduce_fusion.8
  20.2 1.9 collective-permute-start.5
  22.2 7.9 %collective-permute-done.1 = bf16[384,1024]{1,0:T(8,128)(2,1)S(1)} collective-permute-done((bf16[384,1024]{1,0:T(8,128)(2,1)S(1)}, bf16[384,1024]{1,0:T(8,128)(2,1)S(1)}, u32[]{:S(2)}, u32[]{:S(2)}) %collective-permute-start.1) | collective-permute-done | bytes 786464 | tf_op jit(solution)/shard_map/ppermute | solution.py:11
  30.1 2.5 collective-permute-start.2
  32.5 0.7 fusion.56
  33.2 0.3 exponential_reduce_fusion.7
  33.5 0.0 collective-permute-done.5
  33.5 1.9 collective-permute-start.6
  35.5 12.1 %collective-permute-done.2 = bf16[384,1024]{1,0:T(8,128)(2,1)S(1)} collective-permute-done((bf16[384,1024]{1,0:T(8,128)(2,1)S(1)}, bf16[384,1024]{1,0:T(8,128)(2,1)S(1)}, u32[]{:S(2)}, u32[]{:S(2)}) %collective-permute-start.2) | collective-permute-done | bytes 786464 | tf_op jit(solution)/shard_map/ppermute | solution.py:11
  47.6 1.9 collective-permute-start.3
  49.5 0.7 fusion.57
  50.2 0.3 exponential_reduce_fusion.6
  50.5 1.9 collective-permute-start.7
  52.4 12.7 %collective-permute-done.3 = bf16[384,1024]{1,0:T(8,128)(2,1)S(1)} collective-permute-done((bf16[384,1024]{1,0:T(8,128)(2,1)S(1)}, bf16[384,1024]{1,0:T(8,128)(2,1)S(1)}, u32[]{:S(2)}, u32[]{:S(2)}) %collective-permute-start.3) | collective-permute-done | bytes 786464 | tf_op jit(solution)/shard_map/ppermute | solution.py:11
  65.1 0.7 fusion.58
  65.8 0.3 exponential_reduce_fusion.5
  66.1 0.8 collective-permute-done.7
  66.9 14.9 %collective-permute-start.9 = (f32[384]{0:T(512)S(1)}, f32[384]{0:T(512)S(1)}, u32[]{:S(2)}, u32[]{:S(2)}) collective-permute-start(f32[384]{0:T(512)S(1)} %add_select_fusion), channel_id=1, source_target_pairs={{0,510},{2,0},{4,2},{6,4},{8,6},{10,8},{12,10},{14,12},{16,14},{18... | collective-permute-start | bytes 4616 | tf_op jit(solution)/shard_map/ppermute | solution.py:11
  81.9 0.8 collective-permute-done.9
  82.7 2.4 collective-permute-start.11
  85.1 2.5 collective-permute-done.11
  87.6 6.6 %collective-permute-start.13 = (f32[384]{0:T(512)S(1)}, f32[384]{0:T(512)S(1)}, u32[]{:S(2)}, u32[]{:S(2)}) collective-permute-start(f32[384]{0:T(512)S(1)} %collective-permute-done.11), channel_id=1, source_target_pairs={{0,510},{2,0},{4,2},{6,4},{8,6},{10,8},{12,10},{14,12},{16,14},{18... | collective-permute-start | bytes 4616 | tf_op jit(solution)/shard_map/ppermute | solution.py:11
  94.2 0.8 collective-permute-done.13
  95.0 8.3 %collective-permute-start.15 = (f32[384]{0:T(512)S(1)}, f32[384]{0:T(512)S(1)}, u32[]{:S(2)}, u32[]{:S(2)}) collective-permute-start(f32[384]{0:T(512)S(1)} %collective-permute-done.13), channel_id=1, source_target_pairs={{0,510},{2,0},{4,2},{6,4},{8,6},{10,8},{12,10},{14,12},{16,14},{18... | collective-permute-start | bytes 4616 | tf_op jit(solution)/shard_map/ppermute | solution.py:11
  103.3 3.4 gather_fusion
  106.8 0.0 collective-permute-done.15
  106.8 0.7 subtract_reduce_fusion
  107.5 0.7 fusion.9
  108.2 7.8 %collective-permute-start.16 = (f32[384,1024]{1,0:T(8,128)S(1)}, f32[384,1024]{1,0:T(8,128)S(1)}, u32[]{:S(2)}, u32[]{:S(2)}) collective-permute-start(f32[384,1024]{1,0:T(8,128)S(1)} %fusion.9), channel_id=1, source_target_pairs={{0,510},{2,0},{4,2},{6,4},{8,6},{10,8},{12,10},{14,12},{16,14},{18... | collective-permute-start | bytes 4718600 | tf_op jit(solution)/shard_map/ppermute | solution.py:11
  116.1 5.6 %collective-permute-start.8 = (bf16[384,1024]{1,0:T(8,128)(2,1)S(1)}, bf16[384,1024]{1,0:T(8,128)(2,1)S(1)}, u32[]{:S(2)}, u32[]{:S(2)}) collective-permute-start(bf16[384,1024]{1,0:T(8,128)(2,1)S(1)} %collective-permute-done.3), channel_id=1, source_target_pairs={{0,510},{2,0},{4,2},{6,4},{8,6},{10,8},{12,10},{14,12},{16,14},{18... | collective-permute-start | bytes 2359304 | tf_op jit(solution)/shard_map/ppermute | solution.py:11
  121.7 16.7 %collective-permute-done.8 = bf16[384,1024]{1,0:T(8,128)(2,1)S(1)} collective-permute-done((bf16[384,1024]{1,0:T(8,128)(2,1)S(1)}, bf16[384,1024]{1,0:T(8,128)(2,1)S(1)}, u32[]{:S(2)}, u32[]{:S(2)}) %collective-permute-start.8) | collective-permute-done | bytes 786464 | tf_op jit(solution)/shard_map/ppermute | solution.py:11
  138.4 0.6 convolution_multiply_fusion.3
  139.0 0.0 collective-permute-done.16
  139.0 0.7 convolution_add_fusion
  139.7 9.6 %collective-permute-start.17 = (f32[384,1024]{1,0:T(8,128)S(1)}, f32[384,1024]{1,0:T(8,128)S(1)}, u32[]{:S(2)}, u32[]{:S(2)}) collective-permute-start(f32[384,1024]{1,0:T(8,128)S(1)} %convolution_add_fusion), channel_id=1, source_target_pairs={{0,510},{2,0},{4,2},{6,4},{8,6},{10,8},{12,10},{14,12},{16,14},{18... | collective-permute-start | bytes 4718600 | tf_op jit(solution)/shard_map/ppermute | solution.py:11
  149.4 8.0 %collective-permute-start.10 = (bf16[384,1024]{1,0:T(8,128)(2,1)S(1)}, bf16[384,1024]{1,0:T(8,128)(2,1)}, u32[]{:S(2)}, u32[]{:S(2)}) collective-permute-start(bf16[384,1024]{1,0:T(8,128)(2,1)S(1)} %collective-permute-done.8), channel_id=1, source_target_pairs={{0,510},{2,0},{4,2},{6,4},{8,6},{10,8},{12,10},{14,12},{16,14},{18... | collective-permute-start | bytes 2359304 | tf_op jit(solution)/shard_map/ppermute | solution.py:11
  157.4 12.6 %collective-permute-done.10 = bf16[384,1024]{1,0:T(8,128)(2,1)} collective-permute-done((bf16[384,1024]{1,0:T(8,128)(2,1)S(1)}, bf16[384,1024]{1,0:T(8,128)(2,1)}, u32[]{:S(2)}, u32[]{:S(2)}) %collective-permute-start.10) | collective-permute-done | bytes 786464 | tf_op jit(solution)/shard_map/ppermute | solution.py:11
  170.0 1.7 convolution_multiply_fusion.2
  171.8 1.9 fusion.35
  173.6 13.7 %collective-permute-start.18 = (f32[384,1024]{1,0:T(8,128)}, f32[384,1024]{1,0:T(8,128)}, u32[]{:S(2)}, u32[]{:S(2)}) collective-permute-start(f32[384,1024]{1,0:T(8,128)} %fusion.35), channel_id=1, source_target_pairs={{0,510},{2,0},{4,2},{6,4},{8,6},{10,8},{12,10},{14,12},{16,14},{18... | collective-permute-start | bytes 4718600 | tf_op jit(solution)/shard_map/ppermute | solution.py:11
  187.4 8.1 %collective-permute-start.12 = (bf16[384,1024]{1,0:T(8,128)(2,1)}, bf16[384,1024]{1,0:T(8,128)(2,1)}, u32[]{:S(2)}, u32[]{:S(2)}) collective-permute-start(bf16[384,1024]{1,0:T(8,128)(2,1)} %collective-permute-done.10), channel_id=1, source_target_pairs={{0,510},{2,0},{4,2},{6,4},{8,6},{10,8},{12,10},{14,12},{16,14},{18... | collective-permute-start | bytes 2359304 | tf_op jit(solution)/shard_map/ppermute | solution.py:11
  196.8 1.9 fusion.27
  198.8 5.3 %collective-permute-done.12 = bf16[384,1024]{1,0:T(8,128)(2,1)} collective-permute-done((bf16[384,1024]{1,0:T(8,128)(2,1)}, bf16[384,1024]{1,0:T(8,128)(2,1)}, u32[]{:S(2)}, u32[]{:S(2)}) %collective-permute-start.12) | collective-permute-done | bytes 786464 | tf_op jit(solution)/shard_map/ppermute | solution.py:11
  204.1 18.1 %collective-permute-start.14 = (bf16[384,1024]{1,0:T(8,128)(2,1)}, bf16[384,1024]{1,0:T(8,128)(2,1)S(1)}, u32[]{:S(2)}, u32[]{:S(2)}) collective-permute-start(bf16[384,1024]{1,0:T(8,128)(2,1)} %collective-permute-done.12), channel_id=1, source_target_pairs={{0,510},{2,0},{4,2},{6,4},{8,6},{10,8},{12,10},{14,12},{16,14},{18... | collective-permute-start | bytes 2359304 | tf_op jit(solution)/shard_map/ppermute | solution.py:11
  222.2 1.7 convolution_multiply_fusion.1
  223.9 0.0 copy-start.5
  223.9 3.5 fusion.43
  227.5 8.3 %collective-permute-start.19 = (f32[384,1024]{1,0:T(8,128)}, f32[384,1024]{1,0:T(8,128)}, u32[]{:S(2)}, u32[]{:S(2)}) collective-permute-start(f32[384,1024]{1,0:T(8,128)} %fusion.43), channel_id=1, source_target_pairs={{0,510},{2,0},{4,2},{6,4},{8,6},{10,8},{12,10},{14,12},{16,14},{18... | collective-permute-start | bytes 4718600 | tf_op jit(solution)/shard_map/ppermute | solution.py:11
  235.8 1.8 fusion.30
  237.6 3.0 fusion.33
  240.6 0.0 copy-start.8
  240.6 2.9 multiply_reduce_fusion
  246.8 3.1 fusion.41
  249.9 100.7 %all-reduce = (f32[]{:T(128)}, f32[]{:T(128)}) all-reduce(f32[]{:T(128)S(6)} %add.231, f32[]{:T(128)S(6)} %add.235), channel_id=1, replica_groups=mesh['blk'=256,'rep'=2] {'blk','rep'}, use_global_device_ids=true, to_apply=%region_22.23 | all-reduce | flops 2 | bytes 16 | tf_op jit(solution)/shard_map/psum | solution.py:57
  351.8 4.2 %fusion = bf16[1,384,1024]{2,1,0:T(8,128)(2,1)} fusion(bf16[384,1024]{1,0:T(8,128)(2,1)} %copy-done.8, f32[384,1024]{1,0:T(8,128)} %fusion.41, f32[384,1024]{1,0:T(8,128)} %fusion.33, f32[384,1024]{1,0:T(8,128)S(1)} %fusion.27, f32[384,1024]{1,0:T(8,128)} %fusion.30, f32[]{:T(128)S(6)} %exp.103, f32[384,384]{1,0:T(8,128)S(1)} %copy-done.6, ...), kind=kOutput, calls=%fused_computation.4 | convolution fusion | flops 305528832 | bytes 8457220 | tf_op jit(solution)/shard_map/dot_general | solution.py:48
  356.0 3.0 fusion.1
  (40 shorter events, 0.2 us)
Async XLA Ops:
  0.6 5.8 %copy-start = (bf16[1,384,1024]{2,1,0:T(8,128)(2,1)S(1)}, bf16[1,384,1024]{2,1,0:T(8,128)(2,1)}, u32[]{:S(2)}) copy-start(bf16[1,384,1024]{2,1,0:T(8,128)(2,1)} %param.3) | copy-start | bytes 2359300
  0.6 14.3 %collective-permute-start = (bf16[384,1024]{1,0:T(8,128)(2,1)}, bf16[384,1024]{1,0:T(8,128)(2,1)S(1)}, u32[]{:S(2)}, u32[]{:S(2)}) collective-permute-start(bf16[384,1024]{1,0:T(8,128)(2,1)} %bitcast.69), channel_id=1, source_target_pairs={{0,2},{2,4},{4,6},{6,8},{8,10},{10,12},{12,14},{14,16},{16,18},{18... | collective-permute-start | bytes 2359304 | tf_op jit(solution)/shard_map/ppermute | solution.py:11
  8.5 11.7 %collective-permute-start.4 = (f32[384]{0:T(512)S(1)}, f32[384]{0:T(512)S(1)}, u32[]{:S(2)}, u32[]{:S(2)}) collective-permute-start(f32[384]{0:T(512)S(1)} %log_add_fusion.4), channel_id=1, source_target_pairs={{0,2},{2,4},{4,6},{6,8},{8,10},{10,12},{12,14},{14,16},{16,18},{18... | collective-permute-start | bytes 4616 | tf_op jit(solution)/shard_map/ppermute | solution.py:11
  14.9 15.1 %collective-permute-start.1 = (bf16[384,1024]{1,0:T(8,128)(2,1)S(1)}, bf16[384,1024]{1,0:T(8,128)(2,1)S(1)}, u32[]{:S(2)}, u32[]{:S(2)}) collective-permute-start(bf16[384,1024]{1,0:T(8,128)(2,1)S(1)} %collective-permute-done), channel_id=1, source_target_pairs={{0,2},{2,4},{4,6},{6,8},{8,10},{10,12},{12,14},{14,16},{16,18},{18... | collective-permute-start | bytes 2359304 | tf_op jit(solution)/shard_map/ppermute | solution.py:11
  20.2 13.3 %collective-permute-start.5 = (f32[384]{0:T(512)S(1)}, f32[384]{0:T(512)S(1)}, u32[]{:S(2)}, u32[]{:S(2)}) collective-permute-start(f32[384]{0:T(512)S(1)} %add_select_fusion.3), channel_id=1, source_target_pairs={{0,2},{2,4},{4,6},{6,8},{8,10},{10,12},{12,14},{14,16},{16,18},{18... | collective-permute-start | bytes 4616 | tf_op jit(solution)/shard_map/ppermute | solution.py:11
  30.1 17.5 %collective-permute-start.2 = (bf16[384,1024]{1,0:T(8,128)(2,1)S(1)}, bf16[384,1024]{1,0:T(8,128)(2,1)S(1)}, u32[]{:S(2)}, u32[]{:S(2)}) collective-permute-start(bf16[384,1024]{1,0:T(8,128)(2,1)S(1)} %collective-permute-done.1), channel_id=1, source_target_pairs={{0,2},{2,4},{4,6},{6,8},{8,10},{10,12},{12,14},{14,16},{16,18},{18... | collective-permute-start | bytes 2359304 | tf_op jit(solution)/shard_map/ppermute | solution.py:11
  33.5 16.9 %collective-permute-start.6 = (f32[384]{0:T(512)S(1)}, f32[384]{0:T(512)S(1)}, u32[]{:S(2)}, u32[]{:S(2)}) collective-permute-start(f32[384]{0:T(512)S(1)} %add_select_fusion.2), channel_id=1, source_target_pairs={{0,2},{2,4},{4,6},{6,8},{8,10},{10,12},{12,14},{14,16},{16,18},{18... | collective-permute-start | bytes 4616 | tf_op jit(solution)/shard_map/ppermute | solution.py:11
  47.6 17.5 %collective-permute-start.3 = (bf16[384,1024]{1,0:T(8,128)(2,1)S(1)}, bf16[384,1024]{1,0:T(8,128)(2,1)S(1)}, u32[]{:S(2)}, u32[]{:S(2)}) collective-permute-start(bf16[384,1024]{1,0:T(8,128)(2,1)S(1)} %collective-permute-done.2), channel_id=1, source_target_pairs={{0,2},{2,4},{4,6},{6,8},{8,10},{10,12},{12,14},{14,16},{16,18},{18... | collective-permute-start | bytes 2359304 | tf_op jit(solution)/shard_map/ppermute | solution.py:11
  50.5 16.4 %collective-permute-start.7 = (f32[384]{0:T(512)S(1)}, f32[384]{0:T(512)S(1)}, u32[]{:S(2)}, u32[]{:S(2)}) collective-permute-start(f32[384]{0:T(512)S(1)} %add_select_fusion.1), channel_id=1, source_target_pairs={{0,2},{2,4},{4,6},{6,8},{8,10},{10,12},{12,14},{14,16},{16,18},{18... | collective-permute-start | bytes 4616 | tf_op jit(solution)/shard_map/ppermute | solution.py:11
  65.1 51.0 %copy-start.7 = (bf16[384,1024]{1,0:T(8,128)(2,1)}, bf16[384,1024]{1,0:T(8,128)(2,1)S(1)}, u32[]{:S(2)}) copy-start(bf16[384,1024]{1,0:T(8,128)(2,1)S(1)} %collective-permute-done.3) | copy-start | bytes 2359300
  65.8 42.4 %copy-start.2 = (f32[384,384]{1,0:T(8,128)}, f32[384,384]{1,0:T(8,128)S(1)}, u32[]{:S(2)}) copy-start(f32[384,384]{1,0:T(8,128)S(1)} %get-tuple-element.38) | copy-start | bytes 1769476
  66.9 15.8 %collective-permute-start.9 = (f32[384]{0:T(512)S(1)}, f32[384]{0:T(512)S(1)}, u32[]{:S(2)}, u32[]{:S(2)}) collective-permute-start(f32[384]{0:T(512)S(1)} %add_select_fusion), channel_id=1, source_target_pairs={{0,510},{2,0},{4,2},{6,4},{8,6},{10,8},{12,10},{14,12},{16,14},{18... | collective-permute-start | bytes 4616 | tf_op jit(solution)/shard_map/ppermute | solution.py:11
  82.7 56.3 %copy-start.9 = (f32[384]{0:T(512)}, f32[384]{0:T(512)S(1)}, u32[]{:S(2)}) copy-start(f32[384]{0:T(512)S(1)} %collective-permute-done.9) | copy-start | bytes 4612
  82.7 4.9 %collective-permute-start.11 = (f32[384]{0:T(512)S(1)}, f32[384]{0:T(512)S(1)}, u32[]{:S(2)}, u32[]{:S(2)}) collective-permute-start(f32[384]{0:T(512)S(1)} %collective-permute-done.9), channel_id=1, source_target_pairs={{0,510},{2,0},{4,2},{6,4},{8,6},{10,8},{12,10},{14,12},{16,14},{18... | collective-permute-start | bytes 4616 | tf_op jit(solution)/shard_map/ppermute | solution.py:11
  87.5 84.2 %copy-start.11 = (f32[384]{0:T(512)}, f32[384]{0:T(512)S(1)}, u32[]{:S(2)}) copy-start(f32[384]{0:T(512)S(1)} %collective-permute-done.11) | copy-start | bytes 4612
  87.6 7.4 %collective-permute-start.13 = (f32[384]{0:T(512)S(1)}, f32[384]{0:T(512)S(1)}, u32[]{:S(2)}, u32[]{:S(2)}) collective-permute-start(f32[384]{0:T(512)S(1)} %collective-permute-done.11), channel_id=1, source_target_pairs={{0,510},{2,0},{4,2},{6,4},{8,6},{10,8},{12,10},{14,12},{16,14},{18... | collective-permute-start | bytes 4616 | tf_op jit(solution)/shard_map/ppermute | solution.py:11
  95.0 11.8 %collective-permute-start.15 = (f32[384]{0:T(512)S(1)}, f32[384]{0:T(512)S(1)}, u32[]{:S(2)}, u32[]{:S(2)}) collective-permute-start(f32[384]{0:T(512)S(1)} %collective-permute-done.13), channel_id=1, source_target_pairs={{0,510},{2,0},{4,2},{6,4},{8,6},{10,8},{12,10},{14,12},{16,14},{18... | collective-permute-start | bytes 4616 | tf_op jit(solution)/shard_map/ppermute | solution.py:11
  108.2 30.8 %collective-permute-start.16 = (f32[384,1024]{1,0:T(8,128)S(1)}, f32[384,1024]{1,0:T(8,128)S(1)}, u32[]{:S(2)}, u32[]{:S(2)}) collective-permute-start(f32[384,1024]{1,0:T(8,128)S(1)} %fusion.9), channel_id=1, source_target_pairs={{0,510},{2,0},{4,2},{6,4},{8,6},{10,8},{12,10},{14,12},{16,14},{18... | collective-permute-start | bytes 4718600 | tf_op jit(solution)/shard_map/ppermute | solution.py:11
  116.1 22.3 %collective-permute-start.8 = (bf16[384,1024]{1,0:T(8,128)(2,1)S(1)}, bf16[384,1024]{1,0:T(8,128)(2,1)S(1)}, u32[]{:S(2)}, u32[]{:S(2)}) collective-permute-start(bf16[384,1024]{1,0:T(8,128)(2,1)S(1)} %collective-permute-done.3), channel_id=1, source_target_pairs={{0,510},{2,0},{4,2},{6,4},{8,6},{10,8},{12,10},{14,12},{16,14},{18... | collective-permute-start | bytes 2359304 | tf_op jit(solution)/shard_map/ppermute | solution.py:11
  138.4 11.0 %copy-start.4 = (bf16[384,1024]{1,0:T(8,128)(2,1)}, bf16[384,1024]{1,0:T(8,128)(2,1)S(1)}, u32[]{:S(2)}) copy-start(bf16[384,1024]{1,0:T(8,128)(2,1)S(1)} %collective-permute-done.8) | copy-start | bytes 2359300
  139.7 32.0 %collective-permute-start.17 = (f32[384,1024]{1,0:T(8,128)S(1)}, f32[384,1024]{1,0:T(8,128)S(1)}, u32[]{:S(2)}, u32[]{:S(2)}) collective-permute-start(f32[384,1024]{1,0:T(8,128)S(1)} %convolution_add_fusion), channel_id=1, source_target_pairs={{0,510},{2,0},{4,2},{6,4},{8,6},{10,8},{12,10},{14,12},{16,14},{18... | collective-permute-start | bytes 4718600 | tf_op jit(solution)/shard_map/ppermute | solution.py:11
  149.4 20.6 %collective-permute-start.10 = (bf16[384,1024]{1,0:T(8,128)(2,1)S(1)}, bf16[384,1024]{1,0:T(8,128)(2,1)}, u32[]{:S(2)}, u32[]{:S(2)}) collective-permute-start(bf16[384,1024]{1,0:T(8,128)(2,1)S(1)} %collective-permute-done.8), channel_id=1, source_target_pairs={{0,510},{2,0},{4,2},{6,4},{8,6},{10,8},{12,10},{14,12},{16,14},{18... | collective-permute-start | bytes 2359304 | tf_op jit(solution)/shard_map/ppermute | solution.py:11
  173.6 50.3 %collective-permute-start.18 = (f32[384,1024]{1,0:T(8,128)}, f32[384,1024]{1,0:T(8,128)}, u32[]{:S(2)}, u32[]{:S(2)}) collective-permute-start(f32[384,1024]{1,0:T(8,128)} %fusion.35), channel_id=1, source_target_pairs={{0,510},{2,0},{4,2},{6,4},{8,6},{10,8},{12,10},{14,12},{16,14},{18... | collective-permute-start | bytes 4718600 | tf_op jit(solution)/shard_map/ppermute | solution.py:11
  187.4 16.7 %collective-permute-start.12 = (bf16[384,1024]{1,0:T(8,128)(2,1)}, bf16[384,1024]{1,0:T(8,128)(2,1)}, u32[]{:S(2)}, u32[]{:S(2)}) collective-permute-start(bf16[384,1024]{1,0:T(8,128)(2,1)} %collective-permute-done.10), channel_id=1, source_target_pairs={{0,510},{2,0},{4,2},{6,4},{8,6},{10,8},{12,10},{14,12},{16,14},{18... | collective-permute-start | bytes 2359304 | tf_op jit(solution)/shard_map/ppermute | solution.py:11
  204.1 36.5 %collective-permute-start.14 = (bf16[384,1024]{1,0:T(8,128)(2,1)}, bf16[384,1024]{1,0:T(8,128)(2,1)S(1)}, u32[]{:S(2)}, u32[]{:S(2)}) collective-permute-start(bf16[384,1024]{1,0:T(8,128)(2,1)} %collective-permute-done.12), channel_id=1, source_target_pairs={{0,510},{2,0},{4,2},{6,4},{8,6},{10,8},{12,10},{14,12},{16,14},{18... | collective-permute-start | bytes 2359304 | tf_op jit(solution)/shard_map/ppermute | solution.py:11
  223.9 16.7 %copy-start.1 = (f32[384,384]{1,0:T(8,128)}, f32[384,384]{1,0:T(8,128)S(1)}, u32[]{:S(2)}) copy-start(f32[384,384]{1,0:T(8,128)S(1)} %convolution_multiply_fusion.1) | copy-start | bytes 1769476
  223.9 11.9 %copy-start.5 = (bf16[384,1024]{1,0:T(8,128)(2,1)S(1)}, bf16[384,1024]{1,0:T(8,128)(2,1)}, u32[]{:S(2)}) copy-start(bf16[384,1024]{1,0:T(8,128)(2,1)} %copy-done.4) | copy-start | bytes 2359300
  223.9 11.9 %copy-start.10 = (f32[384]{0:T(512)S(1)}, f32[384]{0:T(512)}, u32[]{:S(2)}) copy-start(f32[384]{0:T(512)} %copy-done.9) | copy-start | bytes 4612
  227.5 10.1 %copy-start.12 = (f32[384]{0:T(512)S(1)}, f32[384]{0:T(512)}, u32[]{:S(2)}) copy-start(f32[384]{0:T(512)} %copy-done.11) | copy-start | bytes 4612
  227.5 128.5 %collective-permute-start.19 = (f32[384,1024]{1,0:T(8,128)}, f32[384,1024]{1,0:T(8,128)}, u32[]{:S(2)}, u32[]{:S(2)}) collective-permute-start(f32[384,1024]{1,0:T(8,128)} %fusion.43), channel_id=1, source_target_pairs={{0,510},{2,0},{4,2},{6,4},{8,6},{10,8},{12,10},{14,12},{16,14},{18... | collective-permute-start | bytes 4718600 | tf_op jit(solution)/shard_map/ppermute | solution.py:11
  237.6 3.0 copy-start.3
  240.6 2.9 copy-start.8
  243.6 108.2 %copy-start.6 = (f32[384,384]{1,0:T(8,128)S(1)}, f32[384,384]{1,0:T(8,128)}, u32[]{:S(2)}) copy-start(f32[384,384]{1,0:T(8,128)} %get-tuple-element.39) | copy-start | bytes 1769476
where the time goes:
time: 362 us; the launch traced here: 361 us
  starting transfers between devices  133 us (37%)
  blocking collectives  101 us (28%)
  waiting for transfers between devices  76.7 us (21%)
  matrix products  35.3 us (10%)
  between operations  9.78 us (3%)
    ppermute x20, starting transfers between devices, shifted(): lax.ppermute(array, axis, [(i, (i + by) % peers) for i in range(peers)])  133 us
    psum x1, blocking collectives, body(): loss_total, scale_total = lax.psum((loss_part, scale_sum), ('blk', 'rep'))  101 us
    ppermute x20, waiting for transfers between devices, shifted(): lax.ppermute(array, axis, [(i, (i + by) % peers) for i in range(peers)])  76.7 us
    dot_general x5, matrix products, body(): jnp.dot(rounded, block, preferred_element_type=jnp.float32)  14 us
    dot_general x9, matrix products, pair_scores(): lax.dot_general(left_rows, right_rows, (((1,), (1,)), ((), ())), preferre...  11.5 us
    dot_general x5, matrix products, body(): lax.dot_general(rounded, image_rows, (((0,), (0,)), ((), ())), preferred_...  9.86 us
  transfers between devices with their start and end apart: 20, of which 11 were waited for; matrix products, arithmetic and copies ran while one was open for 9% of the time, Pallas kernels for 0%

commit v1 on v0

v1 whole, which is shorter than its diff:
```python
import functools
import math

import jax
import jax.numpy as jnp
from jax import lax
from jax.experimental import pallas as pl
from jax.experimental.pallas import tpu as pltpu
from jax.sharding import PartitionSpec as P

HOPS = 4
KEYS = HOPS + 1
LOG2E = math.log2(math.e)
LN2 = math.log(2.0)
MESH = pl.DeviceIdType.MESH
PARTS = 3


def kernel(peers, ls_ref, img, txt, gimg, gtxt, loss, gscale,
           X, S, E, G, M, L, W, own_lse, LR, AR, lsem, ssem, rsem, lse_ssem, lse_rsem, ar_ssem, ar_rsem):
    rows = img.shape[1]
    width = img.shape[2]
    piece = rows // PARTS
    b = lax.axis_index("blk")
    rep = lax.axis_index("rep")
    core = lax.rem(b, 2)
    sib = b + 1 - 2 * core
    step = tuple(lax.rem(b + d + peers, peers) for d in (2, -2))
    own = (txt, img)

    low, mid, high = lax.rem(b, 8), lax.rem(b // 8, 8), lax.rem(b // 64, 4) * 2 + rep
    where = (low, mid, high)

    def group_peer(stage, m):
        at = lax.rem(where[stage] + m, 8)
        if stage == 0:
            return (b - low + at, rep)
        if stage == 1:
            return (b + 8 * (at - mid), rep)
        return (lax.rem(b, 64) + 64 * (at // 2), lax.rem(at, 2))

    barrier = pltpu.get_barrier_semaphore()
    near = [lax.rem(b + d + peers, peers) for d in (2, -2, 1, -1, 3, -3, 4, -4)]
    for d in near:
        pl.semaphore_signal(barrier, inc=1, device_id=(d, rep), device_id_type=MESH)
    for stage in range(3):
        for m in range(1, 8):
            pl.semaphore_signal(barrier, inc=1, device_id=group_peer(stage, m), device_id_type=MESH)
    loads = [pltpu.make_async_copy(own[p].at[0], X.at[p, pl.ds(0, rows)], lsem.at[p]) for p in range(2)]
    for load in loads:
        load.start()
    pl.semaphore_wait(barrier, len(near) + 21)

    sends = []

    def send(src, dst, s, r, d):
        copy = pltpu.make_async_remote_copy(
            src_ref=src, dst_ref=dst, send_sem=s, recv_sem=r, device_id=d, device_id_type=MESH)
        copy.start()
        sends.append(copy)

    def at(k, j):
        return pl.ds(rows * k + j * piece, piece)

    def arrived(p, k, j):
        here = X.at[p, at(k, j)]
        pltpu.make_async_remote_copy(
            src_ref=here, dst_ref=here, send_sem=ssem.at[0, 0, 0], recv_sem=rsem.at[p, k, j],
            device_id=(sib, rep), device_id_type=MESH).wait_recv()

    for j in range(PARTS):
        for p in range(2):
            send(own[p].at[0, pl.ds(j * piece, piece)], X.at[p, at(2, j)], ssem.at[0, p, j], rsem.at[p, 2, j], (step[p], rep))
    for load in loads:
        load.wait()
    for j in range(PARTS):
        send(X.at[core, at(0, j)], X.at[core, at(1, j)], ssem.at[1, 0, j], rsem.at[core, 1, j], (sib, rep))

    scale = jnp.exp(jnp.full((1, 1), ls_ref[0], jnp.float32))
    scale2 = scale * LOG2E

    def score(p, first, count, start=False):
        s = scale2 * lax.dot_general(
            X[1 - p, pl.ds(0, rows)], X[p, pl.ds(first, count)], (((1,), (1,)), ((), ())),
            preferred_element_type=jnp.float32)
        S[p, :, pl.ds(first, count)] = s
        top = jnp.max(s, axis=1, keepdims=True)
        if not start:
            old = M[p]
            top = jnp.maximum(top, old)
        e = jnp.exp2(s - top)
        total = jnp.sum(e, axis=1, keepdims=True)
        weighted = jnp.sum(e * s, axis=1, keepdims=True)
        if not start:
            fade = jnp.exp2(old - top)
            total = total + fade * L[p]
            weighted = weighted + fade * W[p]
        M[p], L[p], W[p] = top, total, weighted
        return s

    eye = (lax.broadcasted_iota(jnp.int32, (rows, rows), 0) == lax.broadcasted_iota(jnp.int32, (rows, rows), 1))
    tile = score(0, 0, rows, start=True)
    diag = jnp.sum(jnp.where(eye, tile, 0.0))
    score(1, 0, rows, start=True)

    for j in range(PARTS):
        for p in range(2):
            arrived(p, 2, j)
            send(X.at[p, at(2, j)], X.at[p, at(4, j)], ssem.at[2, p, j], rsem.at[p, 4, j], (step[p], rep))
            k = 3 - 2 * core if p == 0 else 1 + 2 * core
            send(X.at[p, at(2, j)], X.at[p, at(k, j)], ssem.at[3, p, j], rsem.at[p, k, j], (sib, rep))
    for p in range(2):
        score(p, 2 * rows, rows)
    for p in range(2):
        for j in range(PARTS):
            arrived(p, 1, j)
        score(p, rows, rows)
    for j in range(PARTS):
        arrived(1 - core, 3, j)
    score(1 - core, 3 * rows, rows)
    for j in range(PARTS):
        arrived(1 - core, 4, j)
        send(X.at[1 - core, at(4, j)], X.at[1 - core, at(3, j)], ssem.at[1, 1, j], rsem.at[1 - core, 3, j], (sib, rep))
        arrived(core, 4, j)
        for p in range(2):
            score(p, 4 * rows + j * piece, piece)
        arrived(core, 3, j)
        score(core, 3 * rows + j * piece, piece)

    for p in range(2):
        half = M[p] + jnp.log2(L[p]) + 1.0
        M[p] = half
        flat = jnp.broadcast_to(half, (rows, 128)).T[0:8]
        own_lse[p] = flat
        LR[1 - p, :, pl.ds(0, rows)] = flat
        for k in range(1, KEYS):
            there = lax.rem(b + (k if p == 1 else peers - k), peers)
            send(own_lse.at[p], LR.at[1 - p, :, pl.ds(k * rows, rows)], lse_ssem.at[p, k], lse_rsem.at[1 - p, k], (there, rep))

    lse_sum = jnp.sum(M[0] + M[1]) - 2.0 * rows
    pull = jnp.sum(W[0] / L[0] + W[1] / L[1])
    local_loss = lse_sum - 2.0 * diag
    local_scale = 0.5 * pull - diag
    top_row = lax.broadcasted_iota(jnp.int32, (8, 128), 0) == 0
    part = jnp.where(top_row, local_loss, local_scale)

    def share(stage, value):
        mine = AR.at[stage, where[stage]]
        mine[...] = value
        for m in range(1, 8):
            send(mine, mine, ar_ssem.at[stage, m], ar_rsem.at[stage], group_peer(stage, m))

    def gather(stage):
        seven = AR.at[stage, pl.ds(0, 7)]
        pltpu.make_async_remote_copy(
            src_ref=seven, dst_ref=seven, send_sem=ar_ssem.at[stage, 0], recv_sem=ar_rsem.at[stage],
            device_id=(sib, rep), device_id_type=MESH).wait_recv()
        total = AR[stage, 0]
        for i in range(1, 8):
            total = total + AR[stage, i]
        return total

    share(0, part)
    for p in range(2):
        E[p] = jnp.exp2(S[p] - M[p])
    share(1, gather(0))

    out = (gimg, gtxt)
    for p in range(2):
        for k in range(1, KEYS):
            here = LR.at[p, :, pl.ds(k * rows, rows)]
            pltpu.make_async_remote_copy(
                src_ref=here, dst_ref=here, send_sem=lse_ssem.at[p, 0], recv_sem=lse_rsem.at[p, k],
                device_id=(sib, rep), device_id_type=MESH).wait_recv()
        for k in range(KEYS):
            cols = pl.ds(k * rows, rows)
            g = E[p, :, cols] + jnp.exp2(S[p, :, cols] - LR[p, 0:1, cols])
            if k == 0:
                g = g - eye.astype(jnp.float32)
            G[p, :, cols] = g.astype(jnp.bfloat16)
        for n in range(0, width, 256):
            acc = jnp.dot(G[p], X[p, :, pl.ds(n, 256)], preferred_element_type=jnp.float32)
            out[p][0, :, pl.ds(n, 256)] = (scale * acc).astype(jnp.bfloat16)
        if p == 0:
            share(2, gather(1))
    total = gather(2) * (LN2 / (2 * peers * rows))
    loss[0] = 0.5 * total[0, 0]
    gscale[0] = total[1, 0]
    for copy in sends:
        copy.wait_send()


def body(peers, images, texts, log_scale):
    _, rows, width = images.shape
    grad = jax.ShapeDtypeStruct(images.shape, jnp.bfloat16)
    scalar = jax.ShapeDtypeStruct((1,), jnp.float32)
    dma = pltpu.SemaphoreType.DMA
    vmem = pltpu.VMEM
    gimg, gtxt, loss, gscale = pl.pallas_call(
        functools.partial(kernel, peers),
        out_shape=(grad, grad, scalar, scalar),
        in_specs=[pl.BlockSpec(memory_space=pltpu.SMEM)] + [pl.BlockSpec(memory_space=pltpu.HBM)] * 2,
        out_specs=(pl.BlockSpec(memory_space=vmem),) * 2 + (pl.BlockSpec(memory_space=pltpu.SMEM),) * 2,
        scratch_shapes=[
            vmem((2, KEYS * rows, width), jnp.bfloat16),
            vmem((2, rows, KEYS * rows), jnp.float32),
            vmem((2, rows, KEYS * rows), jnp.float32),
            vmem((2, rows, KEYS * rows), jnp.bfloat16),
            vmem((2, rows, 1), jnp.float32),
            vmem((2, rows, 1), jnp.float32),
            vmem((2, rows, 1), jnp.float32),
            vmem((2, 8, rows), jnp.float32),
            vmem((2, 8, KEYS * rows), jnp.float32),
            vmem((3, 8, 8, 128), jnp.float32),
            dma((2,)),
            dma((4, 2, PARTS)),
            dma((2, KEYS, PARTS)),
            dma((2, KEYS)),
            dma((2, KEYS)),
            dma((3, 8)),
            dma((3,)),
        ],
        compiler_params=pltpu.CompilerParams(
            collective_id=0, has_side_effects=True, vmem_limit_bytes=56 * 2**20),
        cost_estimate=pl.CostEstimate(flops=20 * 2 * rows * rows * width, bytes_accessed=4 * rows * width * 2, transcendentals=30 * rows * rows),
        name="band_clip",
    )(log_scale.reshape(1), images, texts)
    return gimg, gtxt, loss.reshape(()), gscale.reshape(())


def solution(mesh):
    placed = (P("rep", "blk", None), P("rep", "blk", None), P())
    return jax.shard_map(
        functools.partial(body, mesh.shape["blk"]),
        mesh=mesh,
        in_specs=placed,
        out_specs=(P("rep", "blk", None), P("rep", "blk", None), P(), P()),
        check_vma=False,
    )
```

time: 362 us -> 81.5 us (0.23)
  starting transfers between devices: 133 us -> 0 us
  blocking collectives: 101 us -> 0 us
  waiting for transfers between devices: 76.7 us -> 0 us
  Pallas kernels: 0 us -> 73.5 us
  matrix products: 35.3 us -> 0 us
  between operations: 9.78 us -> 4.82 us
    ppermute x20 -> x0, starting transfers between devices: 133 us -> none  [shifted(): lax.ppermute(array, axis, [(i, (i + by) % peers) for i in range(peers)])]
    psum x1 -> x0, blocking collectives: 101 us -> none  [body(): loss_total, scale_total = lax.psum((loss_part, scale_sum), ('blk', 'rep'))]
    ppermute x20 -> x0, waiting for transfers between devices: 76.7 us -> none  [shifted(): lax.ppermute(array, axis, [(i, (i + by) % peers) for i in range(peers)])]
    pallas_call x0 -> x1, Pallas kernels: none -> 73.5 us  [body(): pl.pallas_call(functools.partial(kernel, peers), out_shape=(grad, grad, s...]
    dot_general x19 -> x0, matrix products: 35.3 us -> none  [the longest x5 14 us: body(): jnp.dot(rounded, block, preferred_element_type=jnp.float32)]
  transfers between devices with their start and end apart: 20 -> 0, of which waited for: 11 -> 0; matrix products, arithmetic and copies ran while one was open for 9% -> 0% of each run, Pallas kernels for 0% -> 0%
where the time goes in v1:
time: 81.5 us; the launch traced here: 81.3 us
  Pallas kernels  73.5 us (90%)
  between operations  4.82 us (6%)
  local copies, waits for them, and re-layouts  3.02 us (4%)
    pallas_call x1, Pallas kernels, body(): pl.pallas_call(functools.partial(kernel, peers), out_shape=(grad, grad, s...  73.5 us
    unnamed x4, local copies, waits for them, and re-layouts  3.02 us

profile of v1, /device:TPU:1, one launch (start us, length us, event | category | flops | bytes accessed | tf_op | source)
XLA Modules:
  0.0 81.3 jit_solution(15015522109399903156)
XLA Ops:
  1.3 73.5 %band_clip.1 = (bf16[1,384,1024]{2,1,0:T(8,128)(2,1)}, bf16[1,384,1024]{2,1,0:T(8,128)(2,1)}, f32[1]{0:T(128)}, f32[1]{0:T(128)}) custom-call(f32[1]{0:T(128)} %bitcast.3.ls_ref, bf16[1,384,1024]{2,1,0:T(8,128)(2,1)} %img.1, bf16[1,384,1024]{2,1,0:T(8,128)(2,1)} %txt.1), custom_call_target="tpu_custom_call" | custom-call | flops 6039797760 | bytes 3145728 | tf_op jit(solution)/shard_map/band_clip/pallas_call | solution.py:199
  74.8 0.0 copy-start
  74.8 2.1 %copy.12 = bf16[1,384,1024]{2,1,0:T(8,128)(2,1)} copy(bf16[1,384,1024]{2,1,0:T(8,128)(2,1)} %get-tuple-element.16) | data formatting | bytes 1572864
  76.9 0.0 copy-done
  76.9 0.9 %copy.13 = bf16[1,384,1024]{2,1,0:T(8,128)(2,1)} copy(bf16[1,384,1024]{2,1,0:T(8,128)(2,1)S(1)} %copy-done) | data formatting | bytes 1572864
Async XLA Ops:
  74.8 2.1 %copy-start = (bf16[1,384,1024]{2,1,0:T(8,128)(2,1)S(1)}, bf16[1,384,1024]{2,1,0:T(8,128)(2,1)}, u32[]{:S(2)}) copy-start(bf16[1,384,1024]{2,1,0:T(8,128)(2,1)} %get-tuple-element.17) | copy-start | bytes 2359300

commit v2 on v0

v2 whole, which is shorter than its diff:
```python
import functools
import math

import jax
import jax.numpy as jnp
from jax import lax
from jax.experimental import pallas as pl
from jax.experimental.pallas import tpu as pltpu
from jax.sharding import PartitionSpec as P

HOPS = 4
KEYS = HOPS + 1
LOG2E = math.log2(math.e)
LN2 = math.log(2.0)
MESH = pl.DeviceIdType.MESH
PARTS = 3
HOP_PARTS = 6
LINE = 16
TILE = 128


def kernel(peers, ls_hbm, img, txt, acc0, acc1, sums, ls, acc, X, S, A, lanes, stats, near_part, far_part, LR, AR,
           lsem, ssem, rsem, hop_ssem, hop_rsem, near_ssem, near_rsem, far_ssem, far_rsem, ar_ssem, ar_rsem, known):
    rows, width = img.shape[1], img.shape[2]
    piece = rows // PARTS
    b = lax.axis_index("blk")
    rep = lax.axis_index("rep")
    core = lax.rem(b, 2)
    other = 1 - core
    sib = b + 1 - 2 * core

    def ring(d):
        return (lax.rem(b + d + peers, peers), rep)

    step = (ring(2), ring(-2))
    sibling = (sib, rep)
    own = (txt, img)

    def remote(src, dst, s, r, d):
        return pltpu.make_async_remote_copy(
            src_ref=src, dst_ref=dst, send_sem=s, recv_sem=r, device_id=d, device_id_type=MESH)

    def signal(sem, d):
        pl.semaphore_signal(sem, inc=1, device_id=d, device_id_type=MESH)

    barrier = pltpu.get_barrier_semaphore()
    greeted = (step[0], step[1], sibling, (b, 1 - rep))
    for d in greeted:
        signal(barrier, d)
    loads = [pltpu.make_async_copy(own[p].at[0], X.at[p, pl.ds(0, rows)], lsem.at[p]) for p in range(2)]
    loads.append(pltpu.make_async_copy(ls_hbm, ls, lsem.at[2]))
    for load in loads:
        load.start()
    pl.semaphore_wait(barrier, len(greeted))

    def at(k, j):
        return pl.ds(pl.multiple_of(rows * k + j * piece, piece), piece)

    def arrived(p, k, j):
        here = X.at[p, at(k, j)]
        remote(here, here, ssem.at[0, 0], rsem.at[p, k, j], sibling).wait_recv()

    hop_piece = rows // HOP_PARTS

    def hop_at(k, i):
        return pl.ds(pl.multiple_of(rows * k + i * hop_piece, hop_piece), hop_piece)

    def hopped(p, far, i):
        here = X.at[p, hop_at(2 + 2 * far, i)]
        remote(here, here, hop_ssem.at[0, 0, 0], hop_rsem.at[p, far, i], sibling).wait_recv()

    def forward(i):
        for p in range(2):
            remote(X.at[p, hop_at(2, i)], X.at[p, hop_at(4, i)], hop_ssem.at[p, 1, i], hop_rsem.at[p, 1, i], step[p]).start()

    for i in range(HOP_PARTS):
        for p in range(2):
            remote(own[p].at[0, pl.ds(i * hop_piece, hop_piece)], X.at[p, hop_at(2, i)], hop_ssem.at[p, 0, i], hop_rsem.at[p, 0, i], step[p]).start()
    for load in loads:
        load.wait()
    for j in range(PARTS):
        remote(X.at[core, at(0, j)], X.at[core, at(1, j)], ssem.at[0, j], rsem.at[core, 1, j], sibling).start()

    scale2 = jnp.exp(ls[...]) * LOG2E
    lanes[0] = jnp.full(lanes.shape[1:], -jnp.inf, jnp.float32)
    lanes[1:3] = jnp.zeros((2,) + lanes.shape[1:], jnp.float32)
    acc[...] = jnp.zeros(acc.shape, jnp.float32)

    def logits(qp, qk, kp, first, n):
        return scale2 * lax.dot_general(
            X[qp, pl.ds(pl.multiple_of(qk * rows, TILE), rows)], X[kp, pl.ds(pl.multiple_of(first, TILE), n)],
            (((1,), (1,)), ((), ())), preferred_element_type=jnp.float32)

    def count(a, s):
        parts = [s[:, i:i + TILE] for i in range(0, s.shape[1], TILE)]
        old = lanes[0, a]
        top = functools.reduce(jnp.maximum, parts, old)
        fade = jnp.exp2(old - top)
        total, weighted = fade * lanes[1, a], fade * lanes[2, a]
        for part in parts:
            e = jnp.exp2(part - top)
            total = total + e
            weighted = weighted + e * part
        lanes[0, a], lanes[1, a], lanes[2, a] = top, total, weighted

    def score(p, first, n):
        s = logits(1 - p, 0, p, first, n)
        for i in range(n // TILE):
            S[p, first // TILE + i] = s[:, i * TILE:(i + 1) * TILE]
        count(p, s)

    @pl.loop(0, 2)
    def _(p):
        score(p, 0, rows)

    for j in range(PARTS):
        arrived(other, 1, j)
    score(other, rows, rows)

    def spread(r):
        for d in (4 << r, -(4 << r)):
            signal(known.at[r], ring(d))

    def learn(r):
        pl.semaphore_wait(known.at[r], 2)

    def near_scores(j):
        @pl.loop(0, 2)
        def _(p):
            score(p, 2 * rows + j * piece, piece)

        @pl.loop(0, 2)
        def _(i):
            p = lax.rem(core + i, 2)
            k = 1 + 2 * i

            @pl.when(jnp.logical_or(i == 1, j < PARTS - 1))
            def _():
                arrived(p, k, j)

            score(p, k * rows + j * piece, piece)

    @pl.loop(0, PARTS)
    def _(j):
        per = HOP_PARTS // PARTS
        for p in range(2):
            hopped(p, 0, j * per)

        @pl.when(j == 0)
        def _():
            spread(0)

        for i in range(1, per):
            for p in range(2):
                hopped(p, 0, j * per + i)
        for p in range(2):
            k = 3 - 2 * core if p == 0 else 1 + 2 * core
            remote(X.at[p, at(2, j)], X.at[p, at(k, j)], ssem.at[1 + p, j], rsem.at[p, k, j], sibling).start()

        @pl.when(j == 0)
        def _():
            forward(0)
            learn(0)
            spread(1)

        @pl.when(j == 1)
        def _():
            forward(1)
            learn(1)
            spread(2)

        @pl.when(j < PARTS - 1)
        def _():
            near_scores(j)

    count(3, logits(core, 2, other, 2 * rows, rows))
    arrived(core, 1, PARTS - 1)

    @pl.loop(0, 2)
    def _(i):
        count(2, logits(other, 2, core, (1 + i) * rows, rows))

    def lay(a):
        top = jnp.max(lanes[0, a].T, axis=0, keepdims=True)
        fade = jnp.exp2(lanes[0, a].T - top)
        total = jnp.sum(fade * lanes[1, a].T, axis=0, keepdims=True)
        weighted = jnp.sum(fade * lanes[2, a].T, axis=0, keepdims=True)
        for j in range(PARTS):
            cols = slice(j * piece, (j + 1) * piece)
            stats[a, 0, j:j + 1] = top[:, cols]
            stats[a, 0, PARTS + j:PARTS + j + 1] = total[:, cols]
            stats[a, 1, j:j + 1] = weighted[:, cols]

    for i in range(2):
        lay(3 - i)
    for q in range(2):
        a = 3 - core if q == 0 else 2 + core
        far_part[q, 2] = stats[a]
        for k in (0, 1, 3, 4):
            there = ring(k - 2 if q == 0 else 2 - k)
            part = pl.ds(0, 2 if k == 0 else 1)
            remote(stats.at[a, part], far_part.at[q, k, part], far_ssem.at[q, k], far_rsem.at[q, k], there).start()
    near_scores(PARTS - 1)
    for p in range(2):
        lay(p)
        near_part[1 - p, 0] = stats[p]
    for q in range(2):
        for k in range(1, KEYS):
            part = pl.ds(0, 1)
            remote(stats.at[1 - q, part], near_part.at[q, k, part], near_ssem.at[q, k], near_rsem.at[q, k], ring(k if q == 0 else -k)).start()
    forward(2)
    learn(2)
    spread(3)
    diag = jnp.zeros((), jnp.float32)
    one = (lax.broadcasted_iota(jnp.int32, (piece, piece), 0) == lax.broadcasted_iota(jnp.int32, (piece, piece), 1)).astype(jnp.float32)
    for j in range(PARTS):
        diag = diag + jnp.sum(S[0, j, pl.ds(j * piece, piece), :] * one)

    def merge(q, k):
        m1, m2 = near_part[q, k, 0, 0:PARTS], far_part[q, k, 0, 0:PARTS]
        l1, l2 = near_part[q, k, 0, PARTS:2 * PARTS], far_part[q, k, 0, PARTS:2 * PARTS]
        top = jnp.maximum(m1, m2)
        f1, f2 = jnp.exp2(m1 - top), jnp.exp2(m2 - top)
        total = f1 * l1 + f2 * l2
        half = top + jnp.log2(total) + 1.0
        for j in range(PARTS):
            LR[q, k, j, 0:1] = half[j:j + 1]
        return half, f1, f2, total

    def part_here(here, s, r):
        remote(here, here, s, r, sibling).wait_recv()

    lse_sum = -2.0 * rows
    pull = 0.0
    for q in range(2):
        part_here(far_part.at[q, 0], far_ssem.at[q, 0], far_rsem.at[q, 0])
        half, f1, f2, total = merge(q, 0)
        lse_sum = lse_sum + jnp.sum(half)
        pull = pull + jnp.sum((f1 * near_part[q, 0, 1, 0:PARTS] + f2 * far_part[q, 0, 1, 0:PARTS]) / total)
        for j in range(PARTS):
            A[1 - q, pl.ds(j * piece, piece)] = jnp.broadcast_to(half[j:j + 1], (TILE, piece)).T

    z, xl, y = lax.rem(b // 2, LINE), lax.rem(b // (2 * LINE), 2), b // (4 * LINE)
    x = 2 * rep + xl
    sizes = (LINE, LINE, 2)
    place = (z, 4 * y + x, core)

    def far_first(n):
        return sorted(range(n), key=lambda d: -min(d, n - d))

    def others(stage):
        if stage == 0:
            return [(b + 2 * (lax.rem(z + d, LINE) - z), rep) for d in far_first(LINE) if d]
        if stage == 1:
            found = []
            for dy, dx in sorted(((i, j) for i in range(4) for j in range(4)), key=lambda d: -sum(min(i, 4 - i) for i in d)):
                if dy or dx:
                    ny, nx = lax.rem(y + dy, 4), lax.rem(x + dx, 4)
                    found.append((4 * LINE * ny + 2 * LINE * lax.rem(nx, 2) + lax.rem(b, 2 * LINE), nx // 2))
            return found
        return [sibling]

    def share(stage, value):
        mine = AR.at[stage, place[stage]]
        mine[...] = value
        for d in others(stage):
            remote(mine, mine, ar_ssem.at[stage], ar_rsem.at[stage], d).start()

    def gather(stage):
        rest = AR.at[stage, pl.ds(0, sizes[stage] - 1)]
        remote(rest, rest, ar_ssem.at[stage], ar_rsem.at[stage], sibling).wait_recv()
        value = AR[stage, 0]
        for i in range(1, sizes[stage]):
            value = value + AR[stage, i]
        return value

    top_row = lax.broadcasted_iota(jnp.int32, (8, TILE), 0) == 0
    share(0, jnp.where(top_row, lse_sum - 2.0 * diag, 0.5 * pull - diag))
    for i in range(3, HOP_PARTS):
        forward(i)
    learn(3)
    spread(4)

    def halves(p, k, j, s):
        return jnp.exp2(s - A[p]) + jnp.exp2(s - LR[p, k, j, 0:1])

    for q in range(2):
        for k in range(1, KEYS):
            part = pl.ds(0, 1)
            part_here(near_part.at[q, k, part], near_ssem.at[q, k], near_rsem.at[q, k])
            if k != 2:
                part_here(far_part.at[q, k, part], far_ssem.at[q, k], far_rsem.at[q, k])
            merge(q, k)
    learn(4)
    spread(5)

    row_id = lax.broadcasted_iota(jnp.int32, (rows, piece), 0)
    col_id = lax.broadcasted_iota(jnp.int32, (rows, piece), 1)

    def near(p, k):
        hit = jnp.where(k == 0, 1.0, 0.0)
        g = [halves(p, k, j, S[p, k * PARTS + j]) - jnp.where(row_id == col_id + j * piece, hit, 0.0) for j in range(PARTS)]
        g = jnp.concatenate([t.astype(jnp.bfloat16) for t in g], axis=1)
        acc[p] += jnp.dot(g, X[p, pl.ds(pl.multiple_of(k * rows, TILE), rows)], preferred_element_type=jnp.float32)

    @pl.loop(0, 3)
    def _(k):
        near(0, k)
        near(1, k)

    near(other, 3)

    def far(p, slots, j):
        x = [X[p, at(k, j)] for k in slots]
        x = x[0] if len(x) == 1 else jnp.concatenate(x, axis=0)
        s = scale2 * lax.dot_general(X[1 - p, pl.ds(0, rows)], x, (((1,), (1,)), ((), ())), preferred_element_type=jnp.float32)
        g = [halves(p, k, j, s[:, i * piece:(i + 1) * piece]).astype(jnp.bfloat16) for i, k in enumerate(slots)]
        g = g[0] if len(g) == 1 else jnp.concatenate(g, axis=1)
        acc[p] += jnp.dot(g, x, preferred_element_type=jnp.float32)

    def far_pieces(j):
        per = HOP_PARTS // PARTS
        for i in range(per):
            hopped(other, 1, j * per + i)
        remote(X.at[other, at(4, j)], X.at[other, at(3, j)], ssem.at[3, j], rsem.at[other, 3, j], sibling).start()
        far(other, (4,), j)
        for i in range(per):
            hopped(core, 1, j * per + i)
        arrived(core, 3, j)
        far(core, (3, 4), j)

    @pl.loop(0, PARTS - 1)
    def _(j):
        far_pieces(j)

    learn(5)
    share(1, gather(0))
    far_pieces(PARTS - 1)
    share(2, gather(1))
    scale = jnp.exp(ls[...])
    acc0[0] = scale * acc[0]
    acc1[0] = scale * acc[1]
    unit = LN2 / (2 * peers * rows)
    sums[...] = gather(2) * jnp.where(top_row, 0.5 * unit, unit)

    for j in range(PARTS):
        for kind in range(4):
            here = X.at[0, at(0, 0)]
            remote(here, here, ssem.at[kind, j], rsem.at[0, 0, 0], sibling).wait_send()
    for i in range(HOP_PARTS):
        for p in range(2):
            for far_hop in range(2):
                here = X.at[0, hop_at(0, 0)]
                remote(here, here, hop_ssem.at[p, far_hop, i], hop_rsem.at[0, 0, 0], sibling).wait_send()
    for q in range(2):
        for k in range(KEYS):
            here = stats.at[0, pl.ds(0, 2 if k == 0 else 1)]
            if k != 2:
                remote(here, here, far_ssem.at[q, k], far_rsem.at[q, k], sibling).wait_send()
            if k != 0:
                remote(here, here, near_ssem.at[q, k], near_rsem.at[q, k], sibling).wait_send()
    for stage in range(3):
        rest = AR.at[stage, pl.ds(0, sizes[stage] - 1)]
        remote(rest, rest, ar_ssem.at[stage], ar_rsem.at[stage], sibling).wait_send()


def body(peers, images, texts, log_scale):
    _, rows, width = images.shape
    f32 = jnp.float32
    dma = pltpu.SemaphoreType.DMA
    vmem = pltpu.VMEM
    side = jax.ShapeDtypeStruct((1, rows, width), f32)
    acc0, acc1, sums = pl.pallas_call(
        functools.partial(kernel, peers),
        out_shape=(side, side, jax.ShapeDtypeStruct((8, TILE), f32)),
        in_specs=[pl.BlockSpec(memory_space=pl.ANY)] + [pl.BlockSpec(memory_space=pltpu.HBM)] * 2,
        out_specs=(pl.BlockSpec(memory_space=vmem),) * 3,
        scratch_shapes=[
            vmem((1, 1), f32),
            vmem((2, rows, width), f32),
            vmem((2, KEYS * rows, width), jnp.bfloat16),
            vmem((2, HOPS * PARTS, rows, rows // PARTS), f32),
            vmem((2, rows, TILE), f32),
            vmem((3, 4, rows, TILE), f32),
            vmem((4, 2, 8, TILE), f32),
            vmem((2, KEYS, 2, 8, TILE), f32),
            vmem((2, KEYS, 2, 8, TILE), f32),
            vmem((2, KEYS, PARTS, 8, TILE), f32),
            vmem((3, LINE, 8, TILE), f32),
            dma((3,)),
            dma((4, PARTS)),
            dma((2, KEYS, PARTS)),
            dma((2, 2, HOP_PARTS)),
            dma((2, 2, HOP_PARTS)),
            dma((2, KEYS)),
            dma((2, KEYS)),
            dma((2, KEYS)),
            dma((2, KEYS)),
            dma((3,)),
            dma((3,)),
            pltpu.SemaphoreType.REGULAR((6,)),
        ],
        compiler_params=pltpu.CompilerParams(
            collective_id=0, has_side_effects=True, vmem_limit_bytes=40 * 2**20),
        cost_estimate=pl.CostEstimate(
            flops=23 * 2 * rows * rows * width, bytes_accessed=4 * rows * width * 2, transcendentals=30 * rows * rows),
        name="band_clip",
    )(log_scale.reshape(1, 1), *(pltpu.with_memory_space_constraint(x, pltpu.HBM) for x in (images, texts)))
    return acc0.astype(jnp.bfloat16), acc1.astype(jnp.bfloat16), sums[0, 0], sums[1, 0]


def solution(mesh):
    placed = (P("rep", "blk", None), P("rep", "blk", None), P())
    return jax.shard_map(
        functools.partial(body, mesh.shape["blk"]),
        mesh=mesh,
        in_specs=placed,
        out_specs=(P("rep", "blk", None), P("rep", "blk", None), P(), P()),
        check_vma=False,
    )
```

time: 362 us -> 68.7 us (0.19)
  starting transfers between devices: 133 us -> 0 us
  blocking collectives: 101 us -> 0 us
  waiting for transfers between devices: 76.7 us -> 0 us
  Pallas kernels: 0 us -> 64.7 us
  matrix products: 35.3 us -> 0 us
  between operations: 9.78 us -> 1.29 us
    ppermute x20 -> x0, starting transfers between devices: 133 us -> none  [shifted(): lax.ppermute(array, axis, [(i, (i + by) % peers) for i in range(peers)])]
    psum x1 -> x0, blocking collectives: 101 us -> none  [body(): loss_total, scale_total = lax.psum((loss_part, scale_sum), ('blk', 'rep'))]
    ppermute x20 -> x0, waiting for transfers between devices: 76.7 us -> none  [shifted(): lax.ppermute(array, axis, [(i, (i + by) % peers) for i in range(peers)])]
    pallas_call x0 -> x1, Pallas kernels: none -> 64.7 us  [body(): pl.pallas_call(functools.partial(kernel, peers), out_shape=(side, side, j...]
    dot_general x19 -> x0, matrix products: 35.3 us -> none  [the longest x5 14 us: body(): jnp.dot(rounded, block, preferred_element_type=jnp.float32)]
  transfers between devices with their start and end apart: 20 -> 0, of which waited for: 11 -> 0; matrix products, arithmetic and copies ran while one was open for 9% -> 0% of each run, Pallas kernels for 0% -> 0%
where the time goes in v2:
time: 68.7 us; the launch traced here: 68.5 us
  Pallas kernels  64.7 us (94%)
  other arithmetic  2 us (3%)
  between operations  1.29 us (2%)
    pallas_call x1, Pallas kernels, body(): pl.pallas_call(functools.partial(kernel, peers), out_shape=(side, side, j...  64.7 us

profile of v2, /device:TPU:1, one launch (start us, length us, event | category | flops | bytes accessed | tf_op | source)
XLA Modules:
  0.0 68.5 jit_solution(9154241854405743150)
XLA Ops:
  1.3 64.7 %band_clip.1 = (f32[1,384,1024]{2,1,0:T(8,128)S(1)}, f32[1,384,1024]{2,1,0:T(8,128)S(1)}, f32[8,128]{1,0:T(8,128)S(1)}) custom-call(f32[1,1]{1,0:T(1,128)} %bitcast.3.ls_hbm, bf16[1,384,1024]{2,1,0:T(8,128)(2,1)} %img.1, bf16[1,384,1024]{2,1,0:T(8,128)(2,1)} %txt.1), custom_call_target="tpu_custom_call" | custom-call | flops 6945767424 | bytes 3145728 | tf_op jit(solution)/shard_map/band_clip/pallas_call | solution.py:373
  66.0 0.5 fusion
  66.5 1.0 %convert_element_type.6 = bf16[1,384,1024]{2,1,0:T(8,128)(2,1)} convert(f32[1,384,1024]{2,1,0:T(8,128)S(1)} %get-tuple-element.7) | non-fusion elementwise | flops 393216 | bytes 2359296 | tf_op jit(solution)/shard_map/convert_element_type | solution.py:409
  67.5 1.0 %convert_element_type.7 = bf16[1,384,1024]{2,1,0:T(8,128)(2,1)} convert(f32[1,384,1024]{2,1,0:T(8,128)S(1)} %get-tuple-element.8) | non-fusion elementwise | flops 393216 | bytes 2359296 | tf_op jit(solution)/shard_map/convert_element_type | solution.py:409

commit v3 on v2

--- a/solution.py
+++ b/solution.py
@@ -19,7 +19,7 @@
 TILE = 128
 
 
-def kernel(peers, ls_hbm, img, txt, acc0, acc1, sums, ls, acc, X, S, A, lanes, stats, near_part, far_part, LR, AR,
+def kernel(peers, ls_hbm, img, txt, gimg, gtxt, sums, ls, acc, X, S, A, lanes, stats, near_part, far_part, LR, AR,
            lsem, ssem, rsem, hop_ssem, hop_rsem, near_ssem, near_rsem, far_ssem, far_rsem, ar_ssem, ar_rsem, known):
     rows, width = img.shape[1], img.shape[2]
     piece = rows // PARTS
@@ -165,7 +165,8 @@
 
         @pl.when(j == 1)
         def _():
-            forward(1)
+            for i in (1, 2):
+                forward(i)
             learn(1)
             spread(2)
 
@@ -208,7 +209,7 @@
         for k in range(1, KEYS):
             part = pl.ds(0, 1)
             remote(stats.at[1 - q, part], near_part.at[q, k, part], near_ssem.at[q, k], near_rsem.at[q, k], ring(k if q == 0 else -k)).start()
-    forward(2)
+    forward(3)
     learn(2)
     spread(3)
     diag = jnp.zeros((), jnp.float32)
@@ -276,11 +277,10 @@
 
     top_row = lax.broadcasted_iota(jnp.int32, (8, TILE), 0) == 0
     share(0, jnp.where(top_row, lse_sum - 2.0 * diag, 0.5 * pull - diag))
-    for i in range(3, HOP_PARTS):
+    for i in (4, 5):
         forward(i)
     learn(3)
     spread(4)
-
     def halves(p, k, j, s):
         return jnp.exp2(s - A[p]) + jnp.exp2(s - LR[p, k, j, 0:1])
 
@@ -310,36 +310,44 @@
 
     near(other, 3)
 
-    def far(p, slots, j):
-        x = [X[p, at(k, j)] for k in slots]
-        x = x[0] if len(x) == 1 else jnp.concatenate(x, axis=0)
-        s = scale2 * lax.dot_general(X[1 - p, pl.ds(0, rows)], x, (((1,), (1,)), ((), ())), preferred_element_type=jnp.float32)
-        g = [halves(p, k, j, s[:, i * piece:(i + 1) * piece]).astype(jnp.bfloat16) for i, k in enumerate(slots)]
-        g = g[0] if len(g) == 1 else jnp.concatenate(g, axis=1)
-        acc[p] += jnp.dot(g, x, preferred_element_type=jnp.float32)
-
-    def far_pieces(j):
+    def far(j, *sides):
+        keys, grads = [], []
+        for p, slots in sides:
+            x = [X[p, at(k, j)] for k in slots]
+            keys.append(x[0] if len(x) == 1 else jnp.concatenate(x, axis=0))
+        scores = [scale2 * lax.dot_general(X[1 - p, pl.ds(0, rows)], x, (((1,), (1,)), ((), ())), preferred_element_type=jnp.float32)
+                  for (p, _), x in zip(sides, keys)]
+        for (p, slots), s in zip(sides, scores):
+            g = [halves(p, k, j, s[:, i * piece:(i + 1) * piece]).astype(jnp.bfloat16) for i, k in enumerate(slots)]
+            grads.append(g[0] if len(g) == 1 else jnp.concatenate(g, axis=1))
+        for (p, _), g, x in zip(sides, grads, keys):
+            acc[p] += jnp.dot(g, x, preferred_element_type=jnp.float32)
+
+    def far_here(p, j):
         per = HOP_PARTS // PARTS
         for i in range(per):
-            hopped(other, 1, j * per + i)
+            hopped(p, 1, j * per + i)
+
+    def far_relay(j):
+        far_here(other, j)
         remote(X.at[other, at(4, j)], X.at[other, at(3, j)], ssem.at[3, j], rsem.at[other, 3, j], sibling).start()
-        far(other, (4,), j)
-        for i in range(per):
-            hopped(core, 1, j * per + i)
+
+    for j in range(PARTS - 1):
+        far_relay(j)
+        far_here(core, j)
         arrived(core, 3, j)
-        far(core, (3, 4), j)
-
-    @pl.loop(0, PARTS - 1)
-    def _(j):
-        far_pieces(j)
-
+        far(j, (other, (4,)), (core, (3, 4)))
     learn(5)
     share(1, gather(0))
-    far_pieces(PARTS - 1)
+    far_relay(PARTS - 1)
+    far(PARTS - 1, (other, (4,)))
+    far_here(core, PARTS - 1)
+    arrived(core, 3, PARTS - 1)
+    far(PARTS - 1, (core, (3, 4)))
     share(2, gather(1))
     scale = jnp.exp(ls[...])
-    acc0[0] = scale * acc[0]
-    acc1[0] = scale * acc[1]
+    gimg[0] = (scale * acc[0]).astype(jnp.bfloat16)
+    gtxt[0] = (scale * acc[1]).astype(jnp.bfloat16)
     unit = LN2 / (2 * peers * rows)
     sums[...] = gather(2) * jnp.where(top_row, 0.5 * unit, unit)
 
@@ -369,8 +377,8 @@
     f32 = jnp.float32
     dma = pltpu.SemaphoreType.DMA
     vmem = pltpu.VMEM
-    side = jax.ShapeDtypeStruct((1, rows, width), f32)
-    acc0, acc1, sums = pl.pallas_call(
+    side = jax.ShapeDtypeStruct((1, rows, width), jnp.bfloat16)
+    gimg, gtxt, sums = pl.pallas_call(
         functools.partial(kernel, peers),
         out_shape=(side, side, jax.ShapeDtypeStruct((8, TILE), f32)),
         in_specs=[pl.BlockSpec(memory_space=pl.ANY)] + [pl.BlockSpec(memory_space=pltpu.HBM)] * 2,
@@ -406,7 +414,7 @@
             flops=23 * 2 * rows * rows * width, bytes_accessed=4 * rows * width * 2, transcendentals=30 * rows * rows),
         name="band_clip",
     )(log_scale.reshape(1, 1), *(pltpu.with_memory_space_constraint(x, pltpu.HBM) for x in (images, texts)))
-    return acc0.astype(jnp.bfloat16), acc1.astype(jnp.bfloat16), sums[0, 0], sums[1, 0]
+    return gimg, gtxt, sums[0, 0], sums[1, 0]
 
 
 def solution(mesh):

time: 68.7 us -> 65.5 us (0.953)
  Pallas kernels: 64.7 us -> 61.8 us
  other arithmetic: 2 us -> 0 us
  local copies, waits for them, and re-layouts: 0.52 us -> 2.28 us
    pallas_call x1, Pallas kernels: 64.7 us -> 61.8 us  [body(): pl.pallas_call(functools.partial(kernel, peers), out_shape=(side, side, j...]
    convert_element_type x2 -> x0, other arithmetic: 2 us -> none  [the longest x1 1 us: body(): acc0.astype(jnp.bfloat16)]
    unnamed x0 -> x2, local copies, waits for them, and re-layouts: none -> 1.76 us
where the time goes in v3:
time: 65.5 us; the launch traced here: 65.3 us
  Pallas kernels  61.8 us (94%)
  local copies, waits for them, and re-layouts  2.28 us (3%)
  between operations  1.29 us (2%)
    pallas_call x1, Pallas kernels, body(): pl.pallas_call(functools.partial(kernel, peers), out_shape=(side, side, j...  61.8 us
    unnamed x2, local copies, waits for them, and re-layouts  1.76 us

profile of v3, /device:TPU:1, one launch (start us, length us, event | category | flops | bytes accessed | tf_op | source)
XLA Modules:
  0.0 65.3 jit_solution(5625755932204020555)
XLA Ops:
  1.3 61.8 %band_clip.1 = (bf16[1,384,1024]{2,1,0:T(8,128)(2,1)S(1)}, bf16[1,384,1024]{2,1,0:T(8,128)(2,1)S(1)}, f32[8,128]{1,0:T(8,128)S(1)}) custom-call(f32[1,1]{1,0:T(1,128)} %bitcast.3.ls_hbm, bf16[1,384,1024]{2,1,0:T(8,128)(2,1)} %img.1, bf16[1,384,1024]{2,1,0:T(8,128)(2,1)} %txt.1), custom_call_target="tpu_custom_call" | custom-call | flops 6945767424 | bytes 3145728 | tf_op jit(solution)/shard_map/band_clip/pallas_call | solution.py:381
  63.0 0.5 fusion
  63.6 0.9 %copy.10 = bf16[1,384,1024]{2,1,0:T(8,128)(2,1)} copy(bf16[1,384,1024]{2,1,0:T(8,128)(2,1)S(1)} %get-tuple-element.16) | data formatting | bytes 1572864
  64.4 0.9 %copy.11 = bf16[1,384,1024]{2,1,0:T(8,128)(2,1)} copy(bf16[1,384,1024]{2,1,0:T(8,128)(2,1)S(1)} %get-tuple-element.17) | data formatting | bytes 1572864

commit v4 on v3

--- a/solution.py
+++ b/solution.py
@@ -19,7 +19,7 @@
 TILE = 128
 
 
-def kernel(peers, ls_hbm, img, txt, gimg, gtxt, sums, ls, acc, X, S, A, lanes, stats, near_part, far_part, LR, AR,
+def kernel(peers, ls_hbm, img, txt, grads, sums, ls, acc, X, S, A, lanes, stats, near_part, far_part, LR, AR,
            lsem, ssem, rsem, hop_ssem, hop_rsem, near_ssem, near_rsem, far_ssem, far_rsem, ar_ssem, ar_rsem, known):
     rows, width = img.shape[1], img.shape[2]
     piece = rows // PARTS
@@ -210,6 +210,7 @@
             part = pl.ds(0, 1)
             remote(stats.at[1 - q, part], near_part.at[q, k, part], near_ssem.at[q, k], near_rsem.at[q, k], ring(k if q == 0 else -k)).start()
     forward(3)
+    forward(4)
     learn(2)
     spread(3)
     diag = jnp.zeros((), jnp.float32)
@@ -277,8 +278,7 @@
 
     top_row = lax.broadcasted_iota(jnp.int32, (8, TILE), 0) == 0
     share(0, jnp.where(top_row, lse_sum - 2.0 * diag, 0.5 * pull - diag))
-    for i in (4, 5):
-        forward(i)
+    forward(5)
     learn(3)
     spread(4)
     def halves(p, k, j, s):
@@ -311,7 +311,7 @@
     near(other, 3)
 
     def far(j, *sides):
-        keys, grads = [], []
+        keys, weights = [], []
         for p, slots in sides:
             x = [X[p, at(k, j)] for k in slots]
             keys.append(x[0] if len(x) == 1 else jnp.concatenate(x, axis=0))
@@ -319,8 +319,8 @@
                   for (p, _), x in zip(sides, keys)]
         for (p, slots), s in zip(sides, scores):
             g = [halves(p, k, j, s[:, i * piece:(i + 1) * piece]).astype(jnp.bfloat16) for i, k in enumerate(slots)]
-            grads.append(g[0] if len(g) == 1 else jnp.concatenate(g, axis=1))
-        for (p, _), g, x in zip(sides, grads, keys):
+            weights.append(g[0] if len(g) == 1 else jnp.concatenate(g, axis=1))
+        for (p, _), g, x in zip(sides, weights, keys):
             acc[p] += jnp.dot(g, x, preferred_element_type=jnp.float32)
 
     def far_here(p, j):
@@ -337,8 +337,9 @@
         far_here(core, j)
         arrived(core, 3, j)
         far(j, (other, (4,)), (core, (3, 4)))
-    learn(5)
-    share(1, gather(0))
+        if j == 0:
+            learn(5)
+            share(1, gather(0))
     far_relay(PARTS - 1)
     far(PARTS - 1, (other, (4,)))
     far_here(core, PARTS - 1)
@@ -346,8 +347,8 @@
     far(PARTS - 1, (core, (3, 4)))
     share(2, gather(1))
     scale = jnp.exp(ls[...])
-    gimg[0] = (scale * acc[0]).astype(jnp.bfloat16)
-    gtxt[0] = (scale * acc[1]).astype(jnp.bfloat16)
+    for p in range(2):
+        grads[p] = (scale * acc[p]).astype(jnp.bfloat16)
     unit = LN2 / (2 * peers * rows)
     sums[...] = gather(2) * jnp.where(top_row, 0.5 * unit, unit)
 
@@ -377,12 +378,11 @@
     f32 = jnp.float32
     dma = pltpu.SemaphoreType.DMA
     vmem = pltpu.VMEM
-    side = jax.ShapeDtypeStruct((1, rows, width), jnp.bfloat16)
-    gimg, gtxt, sums = pl.pallas_call(
+    grads, sums = pl.pallas_call(
         functools.partial(kernel, peers),
-        out_shape=(side, side, jax.ShapeDtypeStruct((8, TILE), f32)),
+        out_shape=(jax.ShapeDtypeStruct((2, rows, width), jnp.bfloat16), jax.ShapeDtypeStruct((8, TILE), f32)),
         in_specs=[pl.BlockSpec(memory_space=pl.ANY)] + [pl.BlockSpec(memory_space=pltpu.HBM)] * 2,
-        out_specs=(pl.BlockSpec(memory_space=vmem),) * 3,
+        out_specs=(pl.BlockSpec(memory_space=vmem),) * 2,
         scratch_shapes=[
             vmem((1, 1), f32),
             vmem((2, rows, width), f32),
@@ -414,7 +414,7 @@
             flops=23 * 2 * rows * rows * width, bytes_accessed=4 * rows * width * 2, transcendentals=30 * rows * rows),
         name="band_clip",
     )(log_scale.reshape(1, 1), *(pltpu.with_memory_space_constraint(x, pltpu.HBM) for x in (images, texts)))
-    return gimg, gtxt, sums[0, 0], sums[1, 0]
+    return grads[0:1], grads[1:2], sums[0, 0], sums[1, 0]
 
 
 def solution(mesh):

time: 65.5 us -> 64.8 us (0.989)
    unnamed x2 -> x0, local copies, waits for them, and re-layouts: 1.76 us -> none
    slice x1 -> x2, local copies, waits for them, and re-layouts: 0.52 us -> 1.78 us  [body(): return (grads[0:1], grads[1:2], sums[0, 0], sums[1, 0])]
where the time goes in v4:
time: 64.8 us; the launch traced here: 64.6 us
  Pallas kernels  61.6 us (95%)
  local copies, waits for them, and re-layouts  1.78 us (3%)
  between operations  1.29 us (2%)
    pallas_call x1, Pallas kernels, body(): pl.pallas_call(functools.partial(kernel, peers), out_shape=(jax.ShapeDtyp...  61.6 us
    slice x2, local copies, waits for them, and re-layouts, body(): return (grads[0:1], grads[1:2], sums[0, 0], sums[1, 0])  1.78 us

profile of v4, /device:TPU:1, one launch (start us, length us, event | category | flops | bytes accessed | tf_op | source)
XLA Modules:
  0.0 64.6 jit_solution(597001739350563518)
XLA Ops:
  1.3 61.6 %band_clip.1 = (bf16[2,384,1024]{2,1,0:T(8,128)(2,1)S(1)}, f32[8,128]{1,0:T(8,128)S(1)}) custom-call(f32[1,1]{1,0:T(1,128)} %bitcast.3.ls_hbm, bf16[1,384,1024]{2,1,0:T(8,128)(2,1)} %img.1, bf16[1,384,1024]{2,1,0:T(8,128)(2,1)} %txt.1), custom_call_target="tpu_custom_call" | custom-call | flops 6945767424 | bytes 3145728 | tf_op jit(solution)/shard_map/band_clip/pallas_call | solution.py:381
  62.8 1.3 %fusion = (bf16[1,384,1024]{2,1,0:T(8,128)(2,1)}, bf16[1,384,1024]{2,1,0:T(8,128)(2,1)}) fusion(bf16[2,384,1024]{2,1,0:T(8,128)(2,1)S(1)} %get-tuple-element.6), kind=kLoop, calls=%fused_computation | loop fusion | bytes 3145728 | tf_op jit(solution)/shard_map/slice | solution.py:417
  64.1 0.5 fusion.1
